TPU v7x, 512 devices: a whole 4x4x16 slice. The times are simulated.
512 devices in a mesh: sx: 32 (over y, x, core), sy: 16 (over z).
Axes of the slice: x: 4, y: 4, z: 16, core: 2. Of those that a mesh axis runs over, the one named last changes fastest.
Arguments:
- inputs: bfloat16 [65536, 4096], P(('sx', 'sy')), may hold values from -6 to 6
- keys_in: bfloat16 [65536, 128], P(('sx', 'sy')), may hold values from -6 to 6
- queries: bfloat16 [65536, 128], P(('sx', 'sy')), may hold values from -6 to 6
- step_sizes: float32 [65536, 64], P(('sx', 'sy')), may hold values from 0.01 to 0.1
- level_weights: float32 [20, 64], replicated, may hold values from 0.3 to 3
- skip_gain: float32 [64], replicated, may hold values from 0.5 to 1.5
Outputs:
- outputs: bfloat16 [65536, 4096], P(('sx', 'sy'))
All inputs are finite; a program needn't handle non-finite values.
Results may differ from a plain program's by a relative error of at most 0.005.
Values sent between devices are 32-bit elements; how exact they have to be, the bound alone decides.
A program may use at most 64 MiB of HBM per device.

v0:
```python
import jax
import jax.numpy as jnp
from jax import lax
from jax.sharding import PartitionSpec as P

STRETCH = 64


def swapped(block, axis, distance):
    count = lax.axis_size(axis)
    route = []
    for low in range(count):
        high = low | 1 << distance
        if high != low and high < count:
            route += [(low, high), (high, low)]
    return lax.ppermute(block, axis, route)


def add_level(outputs, folded, queries_f32, partner, scale_vec):
    term = partner * scale_vec[None, :]
    return (outputs + jnp.dot(queries_f32, term, precision=lax.Precision.HIGHEST), folded)


def high_levels(
    my_columns, level_weights, index_low, index_high, head_share, head_dim, first_depth, bits_high
):
    high_sum = jnp.zeros_like(my_columns)
    for level_bit in range(bits_high):
        partner = swapped(my_columns, "sx", level_bit)
        upper_half = (index_high // 2**level_bit % 2).astype(jnp.float32)
        level_depth = first_depth + level_bit
        row_share = lax.dynamic_slice_in_dim(
            level_weights[level_depth + 1], index_low * head_share, head_share, 0
        )
        scale_vec = upper_half * jnp.repeat(
            row_share * (2.0**level_depth * STRETCH) ** (-0.5), head_dim
        )
        high_sum = high_sum + partner * scale_vec[None, :]
        my_columns = my_columns + partner
    return high_sum


def on_device(inputs, keys_in, queries, step_sizes, level_weights, skip_gain):
    tok_rows, full_width = inputs.shape
    num_heads = step_sizes.shape[1]
    head_dim = full_width // num_heads
    state_dim = keys_in.shape[1]
    block_count = tok_rows // STRETCH
    local_bits = block_count.bit_length() - 1
    highest = lax.Precision.HIGHEST
    values = (
        (inputs.astype(jnp.float32).reshape(tok_rows, num_heads, head_dim) * step_sizes[:, :, None])
        .reshape(tok_rows, full_width)
        .astype(jnp.bfloat16)
    )
    key_blocks = keys_in.reshape(block_count, STRETCH, state_dim)
    query_blocks = queries.reshape(block_count, STRETCH, state_dim)
    value_blocks = values.reshape(block_count, STRETCH, full_width)
    block_states = jnp.einsum(
        "bcn,bcw->bnw", key_blocks, value_blocks, preferred_element_type=jnp.float32
    )
    scores = jnp.einsum(
        "btn,bsn->bts", query_blocks, key_blocks, preferred_element_type=jnp.float32
    )
    causal = lax.broadcasted_iota(jnp.int32, (STRETCH, STRETCH), 0) >= lax.broadcasted_iota(
        jnp.int32, (STRETCH, STRETCH), 1
    )
    scores = jnp.where(causal[None], scores, 0.0) * STRETCH ** (-0.5)
    intra_weights = (scores[:, None] * level_weights[0][None, :, None, None]).astype(jnp.bfloat16)
    intra_out = jnp.einsum(
        "bhts,bshp->bthp",
        intra_weights,
        value_blocks.reshape(block_count, STRETCH, num_heads, head_dim),
        preferred_element_type=jnp.float32,
    ).reshape(tok_rows, full_width)
    outputs = inputs.astype(jnp.float32) * jnp.repeat(skip_gain, head_dim)[None, :] + intra_out
    queries_f32 = queries.astype(jnp.float32)
    level_bit = 0
    half_span = 2**level_bit
    groups = block_count // (2 * half_span)
    lower_sum = block_states.reshape(groups, 2, half_span, state_dim, full_width)[:, 0].sum(axis=1)
    scale_vec = jnp.repeat(level_weights[level_bit + 1] * (half_span * STRETCH) ** (-0.5), head_dim)
    upper_rows = queries_f32.reshape(groups, 2, half_span * STRETCH, state_dim)[:, 1]
    level_part = jnp.einsum(
        "gtn,gnw->gtw", upper_rows, lower_sum * scale_vec[None, None, :], precision=highest
    )
    outputs = outputs + jnp.stack([jnp.zeros_like(level_part), level_part], axis=1).reshape(
        tok_rows, full_width
    )
    size_low = lax.axis_size("sy")
    size_high = lax.axis_size("sx")
    bits_low = size_low.bit_length() - 1
    bits_high = size_high.bit_length() - 1
    index_low = lax.axis_index("sy")
    index_high = lax.axis_index("sx")
    head_share = num_heads // size_low
    share_width = head_share * head_dim
    group_sum = block_states.sum(axis=0)
    folded = jnp.zeros((state_dim, full_width), jnp.float32)
    for level_bit in range(bits_low):
        partner = swapped(group_sum, "sy", level_bit)
        upper_half = (index_low // 2**level_bit % 2).astype(jnp.float32)
        level_depth = local_bits + level_bit
        scale_vec = upper_half * jnp.repeat(
            level_weights[level_depth + 1] * (2.0**level_depth * STRETCH) ** (-0.5), head_dim
        )
        outputs, folded = add_level(outputs, folded, queries_f32, partner, scale_vec)
        group_sum = group_sum + partner
    my_columns = lax.dynamic_slice_in_dim(group_sum, index_low * share_width, share_width, 1)
    high_sum = high_levels(
        my_columns,
        level_weights,
        index_low,
        index_high,
        head_share,
        head_dim,
        local_bits + bits_low,
        bits_high,
    )
    outputs = outputs + jnp.dot(
        queries_f32,
        lax.all_gather(high_sum, "sy", axis=1, tiled=True),
        precision=lax.Precision.HIGHEST,
    )
    return outputs.astype(jnp.bfloat16)


def solution(mesh):
    placed = (
        P(("sx", "sy"), None),
        P(("sx", "sy"), None),
        P(("sx", "sy"), None),
        P(("sx", "sy"), None),
        P(),
        P(),
    )
    return jax.shard_map(
        on_device, mesh=mesh, in_specs=placed, out_specs=P(("sx", "sy"), None), check_vma=False
    )
```

profile of v0, /device:TPU:1, one launch (start us, length us, event | category | flops | bytes accessed | tf_op | source)
XLA Modules:
  0.0 702.7 jit_solution(6802354924683908111)
XLA Ops:
  6.5 1.6 copy.19
  8.2 0.2 fusion.8
  8.4 0.5 copy.23
  9.0 3.0 bitcast_reduce_fusion
  12.0 4.4 collective-permute-start
  16.4 40.8 %collective-permute-done = f32[128,4096]{0,1:T(8,128)S(1)} collective-permute-done((f32[128,4096]{0,1:T(8,128)S(1)}, f32[128,4096]{0,1:T(8,128)S(1)}, u32[]{:S(2)}, u32[]{:S(2)}) %collective-permute-start) | collective-permute-done | bytes 2097184 | tf_op jit(solution)/shard_map/ppermute | solution.py:16
  57.1 1.4 copy-done.5
  58.5 0.2 add.110
  58.7 9.4 %collective-permute-start.1 = (f32[128,4096]{0,1:T(8,128)S(1)}, f32[128,4096]{0,1:T(8,128)S(1)}, u32[]{:S(2)}, u32[]{:S(2)}) collective-permute-start(f32[128,4096]{0,1:T(8,128)S(1)} %add.110), channel_id=1, source_target_pairs={{0,2},{2,0},{1,3},{3,1},{4,6},{6,4},{5,7},{7,5},{8,10},{10,8},{9,1... | collective-permute-start | bytes 6291464 | tf_op jit(solution)/shard_map/ppermute | solution.py:16
  68.1 90.0 %collective-permute-done.1 = f32[128,4096]{0,1:T(8,128)S(1)} collective-permute-done((f32[128,4096]{0,1:T(8,128)S(1)}, f32[128,4096]{0,1:T(8,128)S(1)}, u32[]{:S(2)}, u32[]{:S(2)}) %collective-permute-start.1) | collective-permute-done | bytes 2097184 | tf_op jit(solution)/shard_map/ppermute | solution.py:16
  158.1 0.2 add.113
  158.3 1.1 copy-done.1
  159.4 8.8 %collective-permute-start.2 = (f32[128,4096]{0,1:T(8,128)S(1)}, f32[128,4096]{0,1:T(8,128)S(1)}, u32[]{:S(2)}, u32[]{:S(2)}) collective-permute-start(f32[128,4096]{0,1:T(8,128)S(1)} %add.113), channel_id=1, source_target_pairs={{0,4},{4,0},{1,5},{5,1},{2,6},{6,2},{3,7},{7,3},{8,12},{12,8},{9,1... | collective-permute-start | bytes 6291464 | tf_op jit(solution)/shard_map/ppermute | solution.py:16
  168.3 225.2 %collective-permute-done.2 = f32[128,4096]{0,1:T(8,128)S(1)} collective-permute-done((f32[128,4096]{0,1:T(8,128)S(1)}, f32[128,4096]{0,1:T(8,128)S(1)}, u32[]{:S(2)}, u32[]{:S(2)}) %collective-permute-start.2) | collective-permute-done | bytes 2097184 | tf_op jit(solution)/shard_map/ppermute | solution.py:16
  393.4 1.7 add.116
  395.1 0.3 copy-done.3
  395.4 102.9 %collective-permute-start.3 = (f32[128,4096]{0,1:T(8,128)}, f32[128,4096]{0,1:T(8,128)}, u32[]{:S(2)}, u32[]{:S(2)}) collective-permute-start(f32[128,4096]{0,1:T(8,128)} %add.116), channel_id=1, source_target_pairs={{0,8},{8,0},{1,9},{9,1},{2,10},{10,2},{3,11},{11,3},{4,12},{12,4},... | collective-permute-start | bytes 6291464 | tf_op jit(solution)/shard_map/ppermute | solution.py:16
  498.3 90.9 %collective-permute-done.3 = f32[128,4096]{0,1:T(8,128)} collective-permute-done((f32[128,4096]{0,1:T(8,128)}, f32[128,4096]{0,1:T(8,128)}, u32[]{:S(2)}, u32[]{:S(2)}) %collective-permute-start.3) | collective-permute-done | bytes 2097184 | tf_op jit(solution)/shard_map/ppermute | solution.py:16
  589.2 1.0 dynamic-slice_add_fusion
  590.2 3.2 collective-permute-start.4
  593.4 1.0 collective-permute-done.4
  594.3 3.1 collective-permute-start.5
  597.5 3.5 collective-permute-done.5
  601.0 4.7 collective-permute-start.6
  605.7 2.5 collective-permute-done.6
  608.2 3.2 collective-permute-start.7
  611.4 1.0 multiply_bitcast_fusion.3
  612.6 1.3 collective-permute-done.7
  613.9 5.0 collective-permute-start.8
  619.1 0.1 mul.413
  619.5 0.1 mul.427
  619.9 1.3 collective-permute-done.8
  621.2 0.9 multiply_add_fusion
  622.1 1.8 reshape_reshape.3
  624.9 0.1 fusion.18
  625.0 2.9 convolution_bitcast_fusion.6
  627.9 5.8 copy.26
  633.7 5.4 reshape.209
  639.1 3.0 convolution_bitcast_fusion.5
  642.1 1.5 stack.7
  643.6 3.1 copy.24
  646.7 2.5 convolution_bitcast_fusion.3
  649.1 2.5 convolution_bitcast_fusion.2
  651.6 4.2 convolution_bitcast_fusion.1
  655.8 29.6 %all-gather.2.cloned.1.call-done = f32[128,4096]{0,1:T(8,128)} async-done(((f32[128,256]{0,1:T(8,128)}), f32[128,4096]{0,1:T(8,128)}) %all-gather.2.cloned.1.call-update) | async-done | bytes 2097168 | tf_op jit(solution)/shard_map/all_gather | solution.py:122
  685.4 2.8 convolution_bitcast_fusion
  688.2 5.3 fusion.5
  693.6 2.3 copy.25
  (49 shorter events, 1.9 us)
Async XLA Ops:
  6.5 2.4 copy-start
  6.5 1.6 copy-start.9
  6.5 678.9 %all-gather.2.cloned.1.call-start = ((), (), s32[]{:S(2)}) async-start(), calls=%async_computation | async-start | bytes 2228224 | tf_op jit(solution)/shard_map/all_gather | solution.py:122
  12.0 45.1 %collective-permute-start = (f32[128,4096]{0,1:T(8,128)S(1)}, f32[128,4096]{0,1:T(8,128)S(1)}, u32[]{:S(2)}, u32[]{:S(2)}) collective-permute-start(f32[128,4096]{0,1:T(8,128)S(1)} %get-tuple-element.16), channel_id=1, source_target_pairs={{0,1},{1,0},{2,3},{3,2},{4,5},{5,4},{6,7},{7,6},{8,9},{9,8},{10,11... | collective-permute-start | bytes 6291464 | tf_op jit(solution)/shard_map/ppermute | solution.py:16
  57.1 1.4 copy-start.5
  58.7 99.4 %collective-permute-start.1 = (f32[128,4096]{0,1:T(8,128)S(1)}, f32[128,4096]{0,1:T(8,128)S(1)}, u32[]{:S(2)}, u32[]{:S(2)}) collective-permute-start(f32[128,4096]{0,1:T(8,128)S(1)} %add.110), channel_id=1, source_target_pairs={{0,2},{2,0},{1,3},{3,1},{4,6},{6,4},{5,7},{7,5},{8,10},{10,8},{9,1... | collective-permute-start | bytes 6291464 | tf_op jit(solution)/shard_map/ppermute | solution.py:16
  158.1 1.3 copy-start.1
  159.4 234.0 %collective-permute-start.2 = (f32[128,4096]{0,1:T(8,128)S(1)}, f32[128,4096]{0,1:T(8,128)S(1)}, u32[]{:S(2)}, u32[]{:S(2)}) collective-permute-start(f32[128,4096]{0,1:T(8,128)S(1)} %add.113), channel_id=1, source_target_pairs={{0,4},{4,0},{1,5},{5,1},{2,6},{6,2},{3,7},{7,3},{8,12},{12,8},{9,1... | collective-permute-start | bytes 6291464 | tf_op jit(solution)/shard_map/ppermute | solution.py:16
  393.4 2.0 copy-start.3
  395.4 193.8 %collective-permute-start.3 = (f32[128,4096]{0,1:T(8,128)}, f32[128,4096]{0,1:T(8,128)}, u32[]{:S(2)}, u32[]{:S(2)}) collective-permute-start(f32[128,4096]{0,1:T(8,128)} %add.116), channel_id=1, source_target_pairs={{0,8},{8,0},{1,9},{9,1},{2,10},{10,2},{3,11},{11,3},{4,12},{12,4},... | collective-permute-start | bytes 6291464 | tf_op jit(solution)/shard_map/ppermute | solution.py:16
  590.2 4.1 collective-permute-start.4
  594.3 6.6 collective-permute-start.5
  601.0 7.2 %collective-permute-start.6 = (f32[128,256]{0,1:T(8,128)S(1)}, f32[128,256]{0,1:T(8,128)S(1)}, u32[]{:S(2)}, u32[]{:S(2)}) collective-permute-start(f32[128,256]{0,1:T(8,128)S(1)} %add.126), channel_id=1, source_target_pairs={{0,64},{64,0},{16,80},{80,16},{32,96},{96,32},{48,112},{112,48},{1... | collective-permute-start | bytes 393224 | tf_op jit(solution)/shard_map/ppermute | solution.py:16
  608.2 5.7 collective-permute-start.7
  613.9 7.2 %collective-permute-start.8 = (f32[128,256]{0,1:T(8,128)S(1)}, f32[128,256]{0,1:T(8,128)S(1)}, u32[]{:S(2)}, u32[]{:S(2)}) collective-permute-start(f32[128,256]{0,1:T(8,128)S(1)} %add.132), channel_id=1, source_target_pairs={{0,256},{256,0},{16,272},{272,16},{32,288},{288,32},{48,304},{304,... | collective-permute-start | bytes 393224 | tf_op jit(solution)/shard_map/ppermute | solution.py:16
  619.9 4.8 copy-start.10
  619.9 5.0 copy-start.8
  643.6 3.1 copy-start.2
  646.7 2.5 copy-start.4
  655.8 32.4 %copy-start.6 = (f32[128,4096]{0,1:T(8,128)S(1)}, f32[128,4096]{0,1:T(8,128)}, u32[]{:S(2)}) copy-start(f32[128,4096]{0,1:T(8,128)} %copy-done.5) | copy-start | bytes 6291460
  685.4 2.8 copy-start.7
Sparse Core Ops, SparseCore 0:
  622.2 63.1 all-gather.1
where the time goes:
time: 712 us; the launch traced here: 703 us
  waiting for transfers between devices  486 us (68%)
  starting transfers between devices  145 us (20%)
  local copies, waits for them, and re-layouts  26.5 us (4%)
  matrix products  26.3 us (4%)
  between operations  13.8 us (2%)
    ppermute x9, waiting for transfers between devices, swapped(): return lax.ppermute(block, axis, route)  456 us
    ppermute x9, starting transfers between devices, swapped(): return lax.ppermute(block, axis, route)  145 us
    all_gather x1, waiting for transfers between devices, on_device(): lax.all_gather(high_sum, 'sy', axis=1, tiled=True)  29.6 us
    dot_general x4, matrix products, add_level(): jnp.dot(queries_f32, term, precision=lax.Precision.HIGHEST)  14.5 us
  transfers between devices with their start and end apart: 10, of which 10 were waited for; matrix products, arithmetic and copies ran while one was open for 5% of the time, Pallas kernels for 0%

commit v1 on v0

v1 whole, which is shorter than its diff:
```python
import functools

import jax
import jax.numpy as jnp
from jax import lax
from jax.experimental import pallas as pl
from jax.experimental.pallas import tpu as pltpu
from jax.sharding import PartitionSpec as P

STRETCH = 64
GROUP = 4
CHUNKS = 1
TILE = 512


def arrived(ref, sem):
    pltpu.make_async_copy(ref, ref, sem).wait()


def kernel(
    x_ref, k_ref, q_ref, dt_ref, lw_ref, sg_ref, o_ref,
    vals, state, coef, acc, lhilo,
    in_up, in_down, out_up, out_down, quarter, base,
    cross_in, cross_out, total, high, plane_in, plane_out,
    up_send, up_recv, down_send, down_recv,
    gather_send, gather_recv, spread_send, spread_recv,
    plane_send, plane_recv,
):
    tokens, full = x_ref.shape
    heads = dt_ref.shape[1]
    head_dim = full // heads
    n_state = k_ref.shape[1]
    planes = lax.axis_size("sx")
    bits_high = planes.bit_length() - 1
    part = n_state // GROUP
    piece = part // GROUP
    width = full // CHUNKS
    cell = full // planes
    my_sx = lax.axis_index("sx")
    my_z = lax.axis_index("sy")
    group = my_z // GROUP
    spot = my_z % GROUP

    barrier = pltpu.get_barrier_semaphore()

    @pl.when(spot > 0)
    def _():
        pl.semaphore_signal(barrier, inc=1, device_id={"sy": my_z - 1})

    @pl.when(spot < GROUP - 1)
    def _():
        pl.semaphore_signal(barrier, inc=1, device_id={"sy": my_z + 1})

    for d in range(1, GROUP):
        pl.semaphore_signal(barrier, inc=1, device_id={"sy": (group ^ d) * GROUP + spot})

    def greet(d, carry):
        pl.semaphore_signal(barrier, inc=1, device_id={"sx": my_sx ^ d})
        return carry

    lax.fori_loop(1, planes, greet, 0)

    first_head = lax.broadcasted_iota(jnp.int32, (heads, TILE), 0) * head_dim
    lane = lax.broadcasted_iota(jnp.int32, (heads, TILE), 1)
    tile = min(TILE, full)
    rows_lw = lw_ref.shape[0]
    row_id = lax.broadcasted_iota(jnp.int32, (rows_lw, heads), 0)
    factor = jnp.full((rows_lw, heads), STRETCH**-0.5, jnp.float32)
    for level in range(1, rows_lw - 1):
        factor = jnp.where(
            row_id == level + 1, (2.0**level * STRETCH) ** -0.5, factor
        )
    table = lw_ref[...] * factor
    exact = functools.partial(
        jnp.dot, precision=lax.Precision.HIGHEST, preferred_element_type=jnp.float32
    )

    def columns(t):
        return pl.ds(pl.multiple_of(t * tile, tile), tile)

    def spread_map(t):
        col = lane[:, :tile] + t * tile
        start = first_head[:, :tile]
        return jnp.where((col >= start) & (col < start + head_dim), 1.0, 0.0)

    def make_state(t, carry):
        cols = columns(t)
        dt = exact(dt_ref[...], spread_map(t))
        v = (x_ref[:, cols].astype(jnp.float32) * dt).astype(jnp.bfloat16)
        vals[:, cols] = v
        state[:, cols] = lax.dot_general(
            k_ref[...], v, (((0,), (0,)), ((), ())), preferred_element_type=jnp.float32
        )
        coef[0:rows_lw, cols] = exact(table, spread_map(t))
        return carry

    lax.fori_loop(0, full // tile, make_state, 0)

    friends = (
        jnp.where(spot > 0, 1, 0) + jnp.where(spot < GROUP - 1, 1, 0) + (GROUP - 1) + (planes - 1)
    )
    pl.semaphore_wait(barrier, friends)

    def chunk(c):
        return pl.ds(c * width, width)

    def rows_of(j):
        return pl.ds(j * part, part)

    def send_up(c, slot, src):
        pltpu.make_async_remote_copy(
            src_ref=src, dst_ref=in_up.at[slot, :, chunk(c)],
            send_sem=up_send.at[c, slot], recv_sem=up_recv.at[c, slot],
            device_id={"sy": my_z + 1},
        ).start()

    def send_down(c, slot, src):
        pltpu.make_async_remote_copy(
            src_ref=src, dst_ref=in_down.at[slot, :, chunk(c)],
            send_sem=down_send.at[c, slot], recv_sem=down_recv.at[c, slot],
            device_id={"sy": my_z - 1},
        ).start()

    def wait_up(c, slot):
        arrived(in_up.at[slot, :, chunk(c)], up_recv.at[c, slot])

    def wait_down(c, slot):
        arrived(in_down.at[slot, :, chunk(c)], down_recv.at[c, slot])

    def st(c, j):
        return state[rows_of(j), chunk(c)]

    def up(c, slot):
        return in_up[slot, :, chunk(c)]

    def down(c, slot):
        return in_down[slot, :, chunk(c)]

    def bs(c):
        return base[:, chunk(c)]

    def weight(row, c):
        return coef[row : row + 1, chunk(c)]

    def early_start(c):
        @pl.when(spot == 0)
        def _():
            for j in (3, 2, 1, 0):
                send_up(c, j, state.at[rows_of(j), chunk(c)])

        @pl.when(spot == 2)
        def _():
            send_up(c, 4, state.at[rows_of(3), chunk(c)])

        @pl.when(spot == 3)
        def _():
            for j in (0, 1, 2):
                send_down(c, j, state.at[rows_of(j), chunk(c)])

    def early_rest(c):
        @pl.when(spot == 0)
        def _():
            wait_down(c, 0)
            quarter[:, chunk(c)] = st(c, 0) + down(c, 0)

        @pl.when(spot == 1)
        def _():
            wait_up(c, 3)
            out_up[3, :, chunk(c)] = st(c, 3) + up(c, 3)
            send_up(c, 3, out_up.at[3, :, chunk(c)])
            wait_down(c, 0)
            out_down[0, :, chunk(c)] = st(c, 0) + down(c, 0)
            send_down(c, 0, out_down.at[0, :, chunk(c)])
            wait_up(c, 2)
            out_up[2, :, chunk(c)] = st(c, 2) + up(c, 2)
            send_up(c, 2, out_up.at[2, :, chunk(c)])
            wait_up(c, 1)
            wait_down(c, 1)
            quarter[:, chunk(c)] = st(c, 1) + up(c, 1) + down(c, 1)

        @pl.when(spot == 2)
        def _():
            wait_down(c, 0)
            out_down[0, :, chunk(c)] = st(c, 0) + down(c, 0)
            send_down(c, 0, out_down.at[0, :, chunk(c)])
            wait_up(c, 3)
            send_up(c, 3, in_up.at[3, :, chunk(c)])
            wait_down(c, 1)
            out_down[1, :, chunk(c)] = st(c, 1) + down(c, 1)
            send_down(c, 1, out_down.at[1, :, chunk(c)])
            wait_up(c, 2)
            wait_down(c, 2)
            quarter[:, chunk(c)] = st(c, 2) + up(c, 2) + down(c, 2)

        @pl.when(spot == 3)
        def _():
            wait_up(c, 4)
            wait_up(c, 3)
            quarter[:, chunk(c)] = st(c, 3) + up(c, 3) + up(c, 4)

    def gather_copy(c, d):
        other = group ^ d
        return pltpu.make_async_remote_copy(
            src_ref=quarter.at[pl.ds(pl.multiple_of(other * piece, piece), piece), chunk(c)],
            dst_ref=cross_in.at[d, :, chunk(c)],
            send_sem=gather_send.at[c, d], recv_sem=gather_recv.at[c, d],
            device_id={"sy": other * GROUP + spot},
        )

    def gather_start(c):
        for d in (2, 1, 3):
            gather_copy(c, d).start()
        cross_in[0, :, chunk(c)] = quarter[
            pl.ds(pl.multiple_of(group * piece, piece), piece), chunk(c)
        ]

    def owner_sx(c, d):
        return ((my_sx // CHUNKS) ^ d) * CHUNKS + c

    def plane_start(c):
        for d in range(1, GROUP):
            arrived(cross_in.at[d, :, chunk(c)], gather_recv.at[c, d])
        total[:, chunk(c)] = (cross_in[0, :, chunk(c)] + cross_in[1, :, chunk(c)]) + (
            cross_in[2, :, chunk(c)] + cross_in[3, :, chunk(c)]
        )

        def cell_of(sx):
            start = c * width + (sx // CHUNKS) * cell
            return pl.ds(pl.multiple_of(start, cell), cell)

        def go(d, carry):
            sx = owner_sx(c, d)

            @pl.when(sx != my_sx)
            def _():
                pltpu.make_async_remote_copy(
                    src_ref=total.at[:, cell_of(sx)], dst_ref=plane_in.at[my_sx],
                    send_sem=plane_send.at[c, 0], recv_sem=plane_recv.at[c, 0],
                    device_id={"sx": sx},
                ).start()

            return carry

        lax.fori_loop(0, planes // CHUNKS, go, 0)

        @pl.when(my_sx % CHUNKS == c)
        def _():
            plane_in[my_sx] = total[:, cell_of(my_sx)]

    def plane_own(c):
        @pl.when(my_sx % CHUNKS == c)
        def _():
            mine = pl.ds(
                pl.multiple_of(c * width + (my_sx // CHUNKS) * cell, cell), cell
            )
            everyone = plane_in.at[pl.ds(0, planes - 1)]
            arrived(everyone, plane_recv.at[c, 0])
            nodes = [[plane_in[s] for s in range(planes)]]
            for level in range(bits_high - 1):
                below = nodes[-1]
                nodes.append([below[2 * n] + below[2 * n + 1] for n in range(len(below) // 2)])
            found = [jnp.zeros((piece, cell), jnp.float32)]
            for level in reversed(range(bits_high)):
                scale = coef[6 + level : 7 + level, mine]
                grown = []
                for n, upper in enumerate(found):
                    grown += [upper, upper + scale * nodes[level][2 * n]]
                found = grown
            for s in range(planes):
                plane_out[s] = found[s]

            def back(d, carry):
                sx = my_sx ^ d
                pltpu.make_async_remote_copy(
                    src_ref=plane_out.at[sx], dst_ref=high.at[:, mine],
                    send_sem=plane_send.at[c, 1], recv_sem=plane_recv.at[c, 1],
                    device_id={"sx": sx},
                ).start()
                return carry

            lax.fori_loop(1, planes, back, 0)
            high[:, mine] = plane_out[my_sx]
            arrived(plane_out.at[pl.ds(0, planes - 1)], plane_send.at[c, 1])

    def spread_copy(c, d):
        return pltpu.make_async_remote_copy(
            src_ref=cross_out.at[d, :, chunk(c)],
            dst_ref=base.at[pl.ds(pl.multiple_of(group * piece, piece), piece), chunk(c)],
            send_sem=spread_send.at[c, d], recv_sem=spread_recv.at[c, d],
            device_id={"sy": (group ^ d) * GROUP + spot},
        )

    def count_cells(c):
        return planes // CHUNKS - jnp.where(my_sx % CHUNKS == c, 1, 0)

    def wait_cells(ref, c, sem):
        cells = planes // CHUNKS

        @pl.when(my_sx % CHUNKS == c)
        def _():
            arrived(ref.at[:, pl.ds(0, (cells - 1) * cell)], sem)

        @pl.when(my_sx % CHUNKS != c)
        def _():
            arrived(ref.at[:, pl.ds(0, cells * cell)], sem)

    def spread_start(c):
        wait_cells(high, c, plane_recv.at[c, 1])
        wait_cells(total, c, plane_send.at[c, 0])
        own = high[:, chunk(c)]
        sums = [cross_in[group ^ g, :, chunk(c)] for g in range(GROUP - 1)]
        w2, w3 = weight(4, c), weight(5, c)
        pair = w3 * (sums[0] + sums[1])
        results = [own, own + w2 * sums[0], own + pair, own + pair + w2 * sums[2]]
        for g in range(GROUP):
            cross_out[group ^ g, :, chunk(c)] = results[g]
        for d in (2, 1, 3):
            spread_copy(c, d).start()
        base[pl.ds(pl.multiple_of(group * piece, piece), piece), chunk(c)] = cross_out[
            0, :, chunk(c)
        ]

    def put(c, j, value):
        high_part = value.astype(jnp.bfloat16)
        low_part = (value - high_part.astype(jnp.float32)).astype(jnp.bfloat16)
        lhilo[rows_of(j), chunk(c)] = high_part
        lhilo[pl.ds(n_state + j * part, part), chunk(c)] = low_part

    def late(c):
        for d in range(1, GROUP):
            other = group ^ d
            arrived(
                base.at[pl.ds(pl.multiple_of(other * piece, piece), piece), chunk(c)],
                spread_recv.at[c, d],
            )
        w0, w1 = weight(2, c), weight(3, c)
        mine = base.at[:, chunk(c)]

        @pl.when(spot == 0)
        def _():
            send_up(c, 4, mine)
            put(c, 0, bs(c))
            for j in (1, 2, 3):
                wait_down(c, j)
                put(c, j, down(c, j))

        @pl.when(spot == 1)
        def _():
            send_down(c, 1, mine)
            out_up[1, :, chunk(c)] = bs(c) + w1 * (st(c, 1) + up(c, 1))
            send_up(c, 1, out_up.at[1, :, chunk(c)])
            put(c, 1, bs(c) + w0 * up(c, 1))
            wait_down(c, 2)
            send_down(c, 2, in_down.at[2, :, chunk(c)])
            wait_up(c, 0)
            wait_up(c, 4)
            out_up[0, :, chunk(c)] = up(c, 4) + w1 * (st(c, 0) + up(c, 0))
            send_up(c, 0, out_up.at[0, :, chunk(c)])
            put(c, 2, down(c, 2) + w0 * up(c, 2))
            put(c, 0, up(c, 4) + w0 * up(c, 0))
            wait_down(c, 3)
            send_down(c, 3, in_down.at[3, :, chunk(c)])
            put(c, 3, down(c, 3) + w0 * up(c, 3))

        @pl.when(spot == 2)
        def _():
            send_down(c, 2, mine)
            level = bs(c) + w1 * up(c, 2)
            out_up[2, :, chunk(c)] = level + w0 * st(c, 2)
            send_up(c, 2, out_up.at[2, :, chunk(c)])
            put(c, 2, level)
            wait_down(c, 3)
            send_down(c, 3, in_down.at[3, :, chunk(c)])
            wait_up(c, 1)
            out_up[1, :, chunk(c)] = up(c, 1) + w0 * st(c, 1)
            send_up(c, 1, out_up.at[1, :, chunk(c)])
            put(c, 1, up(c, 1))
            put(c, 3, down(c, 3) + w1 * up(c, 3))
            wait_up(c, 0)
            out_up[0, :, chunk(c)] = up(c, 0) + w0 * st(c, 0)
            send_up(c, 0, out_up.at[0, :, chunk(c)])
            put(c, 0, up(c, 0))

        @pl.when(spot == 3)
        def _():
            send_down(c, 3, mine)
            put(c, 3, bs(c) + w1 * up(c, 3) + w0 * up(c, 4))
            for j in (2, 1, 0):
                wait_up(c, j)
                put(c, j, up(c, j))

    def local_part():
        scores = lax.dot_general(
            q_ref[...], k_ref[...], (((1,), (1,)), ((), ())), preferred_element_type=jnp.float32
        )
        t_id = lax.broadcasted_iota(jnp.int32, (tokens, tokens), 0)
        s_id = lax.broadcasted_iota(jnp.int32, (tokens, tokens), 1)
        same = (t_id // STRETCH) == (s_id // STRETCH)
        inside = jnp.where(same & (t_id >= s_id), scores, 0.0).astype(jnp.bfloat16)
        before = jnp.where(t_id // STRETCH > s_id // STRETCH, scores, 0.0).astype(jnp.bfloat16)
        gain = jnp.broadcast_to(sg_ref[...], (8, heads))

        def body(t, carry):
            cols = columns(t)
            v = vals[:, cols]
            skip = exact(gain, spread_map(t))[0:1]
            acc[:, cols] = (
                x_ref[:, cols].astype(jnp.float32) * skip
                + coef[0:1, cols] * jnp.dot(inside, v, preferred_element_type=jnp.float32)
                + coef[1:2, cols] * jnp.dot(before, v, preferred_element_type=jnp.float32)
            )
            return carry

        lax.fori_loop(0, full // tile, body, 0)

    def finish():
        q_twice = jnp.concatenate([q_ref[...], q_ref[...]], axis=1)

        def body(t, carry):
            cols = columns(t)
            o_ref[:, cols] = (
                acc[:, cols]
                + jnp.dot(q_twice, lhilo[:, cols], preferred_element_type=jnp.float32)
            ).astype(o_ref.dtype)
            return carry

        lax.fori_loop(0, full // tile, body, 0)

    for c in range(CHUNKS):
        early_start(c)
    local_part()
    for c in range(CHUNKS):
        early_rest(c)
        gather_start(c)
    for c in range(CHUNKS):
        plane_start(c)
    for c in range(CHUNKS):
        plane_own(c)
    for c in range(CHUNKS):
        spread_start(c)
    for c in range(CHUNKS):
        late(c)
    finish()

    for c in range(CHUNKS):
        for d in range(1, GROUP):
            gather_copy(c, d).wait_send()
            spread_copy(c, d).wait_send()

        @pl.when(spot < GROUP - 1)
        def _():
            for slot in range(4):
                arrived(in_up.at[slot, :, chunk(c)], up_send.at[c, slot])

        @pl.when((spot == 0) | (spot == 2))
        def _():
            arrived(in_up.at[4, :, chunk(c)], up_send.at[c, 4])

        @pl.when(spot > 0)
        def _():
            for slot in range(4):
                arrived(in_down.at[slot, :, chunk(c)], down_send.at[c, slot])


def on_device(inputs, keys_in, queries, step_sizes, level_weights, skip_gain):
    tokens, full = inputs.shape
    n_state = keys_in.shape[1]
    planes = lax.axis_size("sx")
    part = n_state // GROUP
    piece = part // GROUP
    f32 = jnp.float32
    vmem = pl.BlockSpec(memory_space=pltpu.VMEM)
    dma = pltpu.SemaphoreType.DMA
    return pl.pallas_call(
        kernel,
        out_shape=jax.ShapeDtypeStruct((tokens, full), jnp.bfloat16),
        in_specs=[vmem] * 6,
        out_specs=vmem,
        scratch_shapes=[
            pltpu.VMEM((tokens, full), jnp.bfloat16),
            pltpu.VMEM((n_state, full), f32),
            pltpu.VMEM((24, full), f32),
            pltpu.VMEM((tokens, full), f32),
            pltpu.VMEM((2 * n_state, full), jnp.bfloat16),
            pltpu.VMEM((5, part, full), f32),
            pltpu.VMEM((4, part, full), f32),
            pltpu.VMEM((4, part, full), f32),
            pltpu.VMEM((2, part, full), f32),
            pltpu.VMEM((part, full), f32),
            pltpu.VMEM((part, full), f32),
            pltpu.VMEM((4, piece, full), f32),
            pltpu.VMEM((4, piece, full), f32),
            pltpu.VMEM((piece, full), f32),
            pltpu.VMEM((piece, full), f32),
            pltpu.VMEM((planes, piece, full // planes), f32),
            pltpu.VMEM((planes, piece, full // planes), f32),
            dma((CHUNKS, 5)), dma((CHUNKS, 5)), dma((CHUNKS, 4)), dma((CHUNKS, 4)),
            dma((CHUNKS, 4)), dma((CHUNKS, 4)), dma((CHUNKS, 4)), dma((CHUNKS, 4)),
            dma((CHUNKS, 2)), dma((CHUNKS, 2)),
        ],
        compiler_params=pltpu.CompilerParams(
            collective_id=0, has_side_effects=True, vmem_limit_bytes=48 * 2**20
        ),
        cost_estimate=pl.CostEstimate(
            flops=10 * tokens * n_state * full, bytes_accessed=4 * tokens * full, transcendentals=0
        ),
    )(inputs, keys_in, queries, step_sizes, level_weights, skip_gain.reshape(1, -1))


def solution(mesh):
    placed = (
        P(("sx", "sy"), None),
        P(("sx", "sy"), None),
        P(("sx", "sy"), None),
        P(("sx", "sy"), None),
        P(),
        P(),
    )
    return jax.shard_map(
        on_device, mesh=mesh, in_specs=placed, out_specs=P(("sx", "sy"), None), check_vma=False
    )
```

time: 712 us -> 152 us (0.21)
  the two profiles are of different devices: /device:TPU:1 before, /device:TPU:96 now
where the time goes in v1:
time: 152 us
  Pallas kernels  149 us (98%)
  local copies, waits for them, and re-layouts  3.1 us (2%)
    pallas_call x1, Pallas kernels, on_device(): pl.pallas_call(kernel, out_shape=jax.ShapeDtypeStruct((tokens, full), jnp...  149 us
    unnamed x12, local copies, waits for them, and re-layouts  3.1 us

profile of v1, /device:TPU:96, one launch (start us, length us, event | category | flops | bytes accessed | tf_op | source)
XLA Modules:
  0.0 152.2 jit_solution(15640565882558805056)
XLA Ops:
  0.0 0.0 copy-start.1
  0.0 0.0 copy-start.2
  0.0 0.0 copy-start.3
  0.0 0.0 copy-start.4
  0.0 0.9 copy.7.dt_ref
  0.9 0.0 copy-done.1
  0.9 0.0 copy-done.2
  0.9 0.0 copy-done.3
  0.9 0.0 copy-done.4
  1.0 0.0 copy-start
  1.0 1.2 copy-done
  2.2 149.1 %shard_map.64 = bf16[128,4096]{1,0:T(8,128)(2,1)S(1)} custom-call(bf16[128,4096]{1,0:T(8,128)(2,1)S(1)} %copy-done, bf16[128,128]{1,0:T(8,128)(2,1)S(1)} %copy-done.1, bf16[128,128]{1,0:T(8,128)(2,1)S(1)} %copy-done.2, f32[128,64]{1,0:T(8,128)S(1)} %copy.7.dt_ref, f32[20,64]{1,0:T(8,128)S(1)} %copy-done.3, f32[1,64]{1,0:T(1,128)S(1)} %bitcast.1), custom_call_target="tpu_custom_call" | custom-call | flops 671088640 | bytes 2097152 | tf_op jit(solution)/shard_map/pallas_call | solution.py:474
  151.2 1.0 copy.9
Async XLA Ops:
  0.0 0.9 copy-start.1
  0.0 0.9 copy-start.2
  0.0 0.9 copy-start.3
  0.0 0.9 copy-start.4
  1.0 1.2 copy-start

commit v2 on v0

v2 whole, which is shorter than its diff:
```python
import functools

import jax
import jax.numpy as jnp
from jax import lax
from jax.experimental import pallas as pl
from jax.experimental.pallas import tpu as pltpu
from jax.sharding import PartitionSpec as P

STRETCH = 64
GROUP = 4
PIECES = 16
HALF = 8
LEAD = 2
TILE = 512
SUM_UP = (14, 12, 10, 8, 15, 13, 11, 9)
SUM_DOWN = (0, 2, 4, 6, 1, 3, 5, 7)
BACK_UP = (6, 4, 2, 0, 7, 5, 3, 1)
BACK_DOWN = (8, 10, 12, 14, 9, 11, 13, 15)


def arrived(ref, sem):
    pltpu.make_async_copy(ref, ref, sem).wait()


def kernel(
    x_ref, k_ref, q_ref, dt_ref, lw_ref, sg_ref, o_ref,
    vals, state, coef, acc, level,
    in_up, in_down, out_up, out_down, base,
    cross_in, cross_out, total, high, plane_in, plane_out,
    up_send, up_recv, down_send, down_recv,
    cross_send, cross_recv, base_recv, plane_send, plane_recv,
):
    tokens, full = x_ref.shape
    heads = dt_ref.shape[1]
    head_dim = full // heads
    n_state = k_ref.shape[1]
    planes = lax.axis_size("sx")
    bits_high = planes.bit_length() - 1
    rows = n_state // PIECES
    cell = full // planes
    tile = min(TILE, full)
    my_sx = lax.axis_index("sx")
    my_z = lax.axis_index("sy")
    group = my_z // GROUP
    spot = my_z % GROUP

    def chip(groups_on, where):
        return {"sy": (group + groups_on) % GROUP * GROUP + where}

    barrier = pltpu.get_barrier_semaphore()

    @pl.when(spot > 0)
    def _():
        pl.semaphore_signal(barrier, inc=1, device_id={"sy": my_z - 1})

    @pl.when(spot < GROUP - 1)
    def _():
        pl.semaphore_signal(barrier, inc=1, device_id={"sy": my_z + 1})

    @pl.when(spot == 0)
    def _():
        for peer in ((2, 3), (3, 0), (3, 3), (1, 0)):
            pl.semaphore_signal(barrier, inc=1, device_id=chip(*peer))

    @pl.when(spot == 3)
    def _():
        for peer in ((2, 0), (1, 3), (1, 0), (3, 3)):
            pl.semaphore_signal(barrier, inc=1, device_id=chip(*peer))

    @pl.when((spot == 0) | (spot == 3))
    def _():
        def greet(d, carry):
            pl.semaphore_signal(barrier, inc=1, device_id={"sx": my_sx ^ d})
            return carry

        lax.fori_loop(1, planes, greet, 0)

    def product(a, b, dims=((1,), (0,))):
        return lax.dot_general(a, b, (dims, ((), ())), preferred_element_type=jnp.float32)

    def columns(t):
        return pl.ds(pl.multiple_of(t * tile, tile), tile)

    shift = (group * (n_state // GROUP) + 5 * n_state // 8) % n_state
    from_id = lax.broadcasted_iota(jnp.int32, (n_state, n_state), 0)
    to_id = lax.broadcasted_iota(jnp.int32, (n_state, n_state), 1)
    turn = jnp.where(from_id == (to_id + shift) % n_state, 1.0, 0.0).astype(jnp.bfloat16)
    k_turned = product(k_ref[...], turn).astype(jnp.bfloat16)

    rows_lw = lw_ref.shape[0]
    row_id = lax.broadcasted_iota(jnp.int32, (rows_lw, heads), 0)
    factor = jnp.full((rows_lw, heads), STRETCH**-0.5, jnp.float32)
    for bit in range(1, rows_lw - 1):
        factor = jnp.where(row_id == bit + 1, (2.0**bit * STRETCH) ** -0.5, factor)
    narrow = jnp.concatenate(
        [dt_ref[...], jnp.broadcast_to(sg_ref[...], (8, heads)), lw_ref[...] * factor], axis=0
    )
    parts = []
    for _ in range(3):
        parts.append(narrow.astype(jnp.bfloat16))
        narrow = narrow - parts[-1].astype(jnp.float32)
    first_head = lax.broadcasted_iota(jnp.int32, (heads, tile), 0) * head_dim
    lane = lax.broadcasted_iota(jnp.int32, (heads, tile), 1)

    def make_state(t, carry):
        cols = columns(t)
        place = lane + t * tile - first_head
        head_map = jnp.where((place >= 0) & (place < head_dim), 1.0, 0.0).astype(jnp.bfloat16)
        wide = product(parts[0], head_map) + product(parts[1], head_map) + product(
            parts[2], head_map
        )
        v = (x_ref[:, cols].astype(jnp.float32) * wide[:tokens]).astype(jnp.bfloat16)
        vals[:, cols] = v
        state[:, cols] = product(k_turned, v, ((0,), (0,)))
        coef[0 : 8 + rows_lw, cols] = wide[tokens:]
        return carry

    lax.fori_loop(0, full // tile, make_state, 0)

    ends = jnp.where((spot == 0) | (spot == 3), 1, 0)
    pl.semaphore_wait(barrier, 2 + ends * (3 + planes - 1))

    def at(p):
        return pl.ds(p * rows, rows)

    def send_up(slot, src):
        pltpu.make_async_remote_copy(
            src_ref=src, dst_ref=in_up.at[slot], send_sem=up_send, recv_sem=up_recv.at[slot],
            device_id={"sy": my_z + 1},
        ).start()

    def send_down(slot, src):
        pltpu.make_async_remote_copy(
            src_ref=src, dst_ref=in_down.at[slot], send_sem=down_send,
            recv_sem=down_recv.at[slot], device_id={"sy": my_z - 1},
        ).start()

    def get_up(slot):
        arrived(in_up.at[slot], up_recv.at[slot])
        return in_up[slot]

    def get_down(slot):
        arrived(in_down.at[slot], down_recv.at[slot])
        return in_down[slot]

    def weight(bit):
        return coef[9 + bit : 10 + bit, :]

    def local_part():
        scores = product(q_ref[...], k_ref[...], ((1,), (1,)))
        t_id = lax.broadcasted_iota(jnp.int32, (tokens, tokens), 0)
        s_id = lax.broadcasted_iota(jnp.int32, (tokens, tokens), 1)
        same = (t_id // STRETCH) == (s_id // STRETCH)
        inside = jnp.where(same & (t_id >= s_id), scores, 0.0).astype(jnp.bfloat16)
        before = jnp.where(t_id // STRETCH > s_id // STRETCH, scores, 0.0).astype(jnp.bfloat16)

        def body(t, carry):
            cols = columns(t)
            v = vals[:, cols]
            acc[:, cols] = (
                x_ref[:, cols].astype(jnp.float32) * coef[0:1, cols]
                + coef[8:9, cols] * product(inside, v)
                + coef[9:10, cols] * product(before, v)
            )
            return carry

        lax.fori_loop(0, full // tile, body, 0)

    def group_sum(p, value):
        half = p % 2
        kind = p // 2
        targets = {
            0: (2, 3, 2), 1: (3, 0, 1), 2: (3, 3, 1),
            5: (1, 0, 3), 6: (1, 3, 3), 7: (2, 0, 2),
        }
        if kind in (3, 4):
            cross_in[half, 0] = value
            return
        groups_on, where, slot = targets[kind]
        out_up[p] = value
        pltpu.make_async_remote_copy(
            src_ref=out_up.at[p], dst_ref=cross_in.at[half, slot],
            send_sem=cross_send, recv_sem=cross_recv.at[half, slot],
            device_id=chip(groups_on, where),
        ).start()

    def cell_of(sx):
        return pl.ds(pl.multiple_of(sx * cell, cell), cell)

    def plane_start(half):
        for slot in range(1, GROUP):
            arrived(cross_in.at[half, slot], cross_recv.at[half, slot])
        total[half] = (cross_in[half, 0] + cross_in[half, 1]) + (
            cross_in[half, 2] + cross_in[half, 3]
        )

        def go(d, carry):
            sx = my_sx ^ d
            pltpu.make_async_remote_copy(
                src_ref=total.at[half, :, cell_of(sx)], dst_ref=plane_in.at[half, my_sx],
                send_sem=plane_send.at[half, 0], recv_sem=plane_recv.at[half, 0],
                device_id={"sx": sx},
            ).start()
            return carry

        lax.fori_loop(1, planes, go, 0)
        plane_in[half, my_sx] = total[half, :, cell_of(my_sx)]

    def plane_own(half):
        mine = cell_of(my_sx)
        arrived(plane_in.at[half, pl.ds(0, planes - 1)], plane_recv.at[half, 0])
        nodes = [[plane_in[half, s] for s in range(planes)]]
        for _ in range(bits_high - 1):
            below = nodes[-1]
            nodes.append([below[2 * n] + below[2 * n + 1] for n in range(len(below) // 2)])
        found = [jnp.zeros((rows, cell), jnp.float32)]
        for bit in reversed(range(bits_high)):
            scale = coef[14 + bit : 15 + bit, mine]
            grown = []
            for n, upper in enumerate(found):
                grown += [upper, upper + scale * nodes[bit][2 * n]]
            found = grown
        for s in range(planes):
            plane_out[half, s] = found[s]

        def back(d, carry):
            sx = my_sx ^ d
            pltpu.make_async_remote_copy(
                src_ref=plane_out.at[half, sx], dst_ref=high.at[half, :, mine],
                send_sem=plane_send.at[half, 1], recv_sem=plane_recv.at[half, 1],
                device_id={"sx": sx},
            ).start()
            return carry

        lax.fori_loop(1, planes, back, 0)
        high[half, :, mine] = plane_out[half, my_sx]

    def spread(half, owner):
        arrived(high.at[half, :, pl.ds(0, (planes - 1) * cell)], plane_recv.at[half, 1])
        own = high[half]
        sums = [cross_in[half, (g - group + GROUP) % GROUP] for g in range(GROUP - 1)]
        w2, w3 = weight(2 + 1), weight(3 + 1)
        pair = w3 * (sums[0] + sums[1])
        results = [own, own + w2 * sums[0], own + pair, own + pair + w2 * sums[2]]
        for g in range(GROUP):
            cross_out[half, (g - group + GROUP) % GROUP] = results[g]
        if owner == 0:
            plan = ((2, 3, 14), (1, 0, 2), (3, 3, 10), (0, 0, 6))
        else:
            plan = ((2, 0, 0), (3, 3, 12), (1, 0, 4), (0, 3, 8))
        for groups_on, where, p in plan:
            slot = (p + half) % HALF
            if groups_on == 0:
                base[slot] = cross_out[half, 0]
            else:
                pltpu.make_async_remote_copy(
                    src_ref=cross_out.at[half, groups_on], dst_ref=base.at[slot],
                    send_sem=cross_send, recv_sem=base_recv.at[slot],
                    device_id=chip(groups_on, where),
                ).start()

    def get_base(p):
        slot = p % HALF
        if p // 2 not in (3, 4):
            arrived(base.at[slot], base_recv.at[slot])
        return base[slot]

    def put(p, value):
        level[at(p), :] = value

    def end_chip(owner, sums, sum_step, later, backs, back_step):
        for p in sums[:6]:
            sum_step(p)
        plane_start(0)
        for p in sums[6:]:
            sum_step(p)
        later(0)
        plane_own(0)
        spread(0, owner)
        plane_start(1)
        for p in backs[:2]:
            back_step(p)
        plane_own(1)
        for p in backs[2:4]:
            back_step(p)
        later(1)
        spread(1, owner)
        for p in backs[4:]:
            back_step(p)

    def in_turn(first, second, lead):
        count = len(first)
        for n in range(count + lead):
            if n < count:
                first[n]()
            if n >= lead:
                second[n - lead]()

    @pl.when(spot == 0)
    def _():
        for p in SUM_UP:
            send_up(p, state.at[at(p)])
        local_part()

        def sum_step(p):
            group_sum(p, state[at(p), :] + get_down(p))

        def later(half):
            for p in BACK_UP[4 * half : 4 * half + 4]:
                send_up(p, state.at[at(p)])

        def back_step(p):
            value = get_base(p)
            send_up(PIECES + p % HALF, base.at[p % HALF])
            put(p, value)

        end_chip(0, SUM_DOWN, sum_step, later, BACK_UP, back_step)
        for r in BACK_DOWN:
            put(r, get_down(r))

    @pl.when(spot == 3)
    def _():
        for p in SUM_DOWN:
            send_down(p, state.at[at(p)])
        local_part()

        def sum_step(p):
            group_sum(p, state[at(p), :] + get_up(p))

        def back_step(r):
            value = get_base(r)
            send_down(r, base.at[r % HALF])
            put(r, value + get_up(PIECES + r % HALF))

        end_chip(3, SUM_UP, sum_step, lambda half: None, BACK_DOWN, back_step)
        for p in BACK_UP:
            put(p, get_up(p))

    w0, w1 = weight(1), weight(2)

    def each(step, order):
        return [functools.partial(step, p) for p in order]

    def sum_up(r):
        out_up[r] = state[at(r), :] + get_up(r)
        send_up(r, out_up.at[r])

    def sum_down(p):
        out_down[p] = state[at(p), :] + get_down(p)
        send_down(p, out_down.at[p])

    @pl.when(spot == 1)
    def _():
        in_turn(each(sum_up, SUM_UP), each(sum_down, SUM_DOWN), LEAD)
        local_part()

        def back_up(p):
            below = get_up(p)
            value = get_up(PIECES + p)
            out_up[p] = value + w1 * (state[at(p), :] + below)
            send_up(p, out_up.at[p])
            put(p, value + w0 * below)

        def back_down(r):
            value = get_down(r)
            send_down(r, in_down.at[r])
            put(r, value + w0 * in_up[r])

        in_turn(each(back_up, BACK_UP), each(back_down, BACK_DOWN), LEAD)

    @pl.when(spot == 2)
    def _():
        in_turn(each(sum_down, SUM_DOWN), each(sum_up, SUM_UP), LEAD)
        for r in BACK_DOWN:
            out_up[HALF + r] = w1 * in_up[r] + w0 * state[at(r), :]
            send_up(HALF + r, out_up.at[HALF + r])
        local_part()

        def back_down(r):
            value = get_down(r)
            send_down(r, in_down.at[r])
            put(r, value + w1 * in_up[r])

        def back_up(p):
            value = get_up(p)
            out_up[p] = value + w0 * state[at(p), :]
            send_up(p, out_up.at[p])
            put(p, value)

        in_turn(each(back_down, BACK_DOWN), each(back_up, BACK_UP), LEAD)

    q_turned = product(q_ref[...], turn).astype(jnp.bfloat16)

    def finish(t, carry):
        cols = columns(t)
        found = level[:, cols]
        high_part = found.astype(jnp.bfloat16)
        low_part = (found - high_part.astype(jnp.float32)).astype(jnp.bfloat16)
        o_ref[:, cols] = (
            acc[:, cols] + product(q_turned, high_part) + product(q_turned, low_part)
        ).astype(o_ref.dtype)
        return carry

    lax.fori_loop(0, full // tile, finish, 0)

    @pl.when((spot == 0) | (spot == 2))
    def _():
        arrived(in_up, up_send)

    @pl.when(spot == 1)
    def _():
        arrived(in_up.at[pl.ds(0, PIECES)], up_send)

    @pl.when(spot > 0)
    def _():
        arrived(in_down, down_send)

    @pl.when((spot == 0) | (spot == 3))
    def _():
        arrived(in_up.at[pl.ds(0, 12)], cross_send)
        for half in range(2):
            for way in range(2):
                arrived(plane_in.at[half, pl.ds(0, planes - 1)], plane_send.at[half, way])


def on_device(inputs, keys_in, queries, step_sizes, level_weights, skip_gain):
    tokens, full = inputs.shape
    n_state = keys_in.shape[1]
    planes = lax.axis_size("sx")
    rows = n_state // PIECES
    f32 = jnp.float32
    vmem = pl.BlockSpec(memory_space=pltpu.VMEM)
    dma = pltpu.SemaphoreType.DMA
    return pl.pallas_call(
        kernel,
        out_shape=jax.ShapeDtypeStruct((tokens, full), jnp.bfloat16),
        in_specs=[vmem] * 6,
        out_specs=vmem,
        scratch_shapes=[
            pltpu.VMEM((tokens, full), jnp.bfloat16),
            pltpu.VMEM((n_state, full), f32),
            pltpu.VMEM((32, full), f32),
            pltpu.VMEM((tokens, full), f32),
            pltpu.VMEM((n_state, full), f32),
            pltpu.VMEM((PIECES + HALF, rows, full), f32),
            pltpu.VMEM((PIECES, rows, full), f32),
            pltpu.VMEM((PIECES + HALF, rows, full), f32),
            pltpu.VMEM((HALF, rows, full), f32),
            pltpu.VMEM((HALF, rows, full), f32),
            pltpu.VMEM((2, GROUP, rows, full), f32),
            pltpu.VMEM((2, GROUP, rows, full), f32),
            pltpu.VMEM((2, rows, full), f32),
            pltpu.VMEM((2, rows, full), f32),
            pltpu.VMEM((2, planes, rows, full // planes), f32),
            pltpu.VMEM((2, planes, rows, full // planes), f32),
            dma, dma((PIECES + HALF,)), dma, dma((PIECES,)),
            dma, dma((2, GROUP)), dma((HALF,)), dma((2, 2)), dma((2, 2)),
        ],
        compiler_params=pltpu.CompilerParams(
            collective_id=0, has_side_effects=True, vmem_limit_bytes=48 * 2**20
        ),
        cost_estimate=pl.CostEstimate(
            flops=10 * tokens * n_state * full, bytes_accessed=4 * tokens * full, transcendentals=0
        ),
    )(inputs, keys_in, queries, step_sizes, level_weights, skip_gain.reshape(1, -1))


def solution(mesh):
    placed = (
        P(("sx", "sy"), None),
        P(("sx", "sy"), None),
        P(("sx", "sy"), None),
        P(("sx", "sy"), None),
        P(),
        P(),
    )
    return jax.shard_map(
        on_device, mesh=mesh, in_specs=placed, out_specs=P(("sx", "sy"), None), check_vma=False
    )
```

time: 712 us -> 133 us (0.19); the launches traced: 703 us -> 132 us
  waiting for transfers between devices: 486 us -> 0 us
  starting transfers between devices: 145 us -> 0 us
  Pallas kernels: 0 us -> 129 us
  matrix products: 26.3 us -> 0 us
  local copies, waits for them, and re-layouts: 26.5 us -> 3.1 us
  between operations: 13.8 us -> 0.07 us
    ppermute x9 -> x0, waiting for transfers between devices: 456 us -> none  [swapped(): return lax.ppermute(block, axis, route)]
    ppermute x9 -> x0, starting transfers between devices: 145 us -> none  [swapped(): return lax.ppermute(block, axis, route)]
    pallas_call x0 -> x1, Pallas kernels: none -> 129 us  [on_device(): pl.pallas_call(kernel, out_shape=jax.ShapeDtypeStruct((tokens, full), jnp...]
    all_gather x1 -> x0, waiting for transfers between devices: 29.6 us -> none  [on_device(): lax.all_gather(high_sum, 'sy', axis=1, tiled=True)]
    dot_general x9 -> x0, matrix products: 26.3 us -> none  [the longest x4 14.5 us: add_level(): jnp.dot(queries_f32, term, precision=lax.Precision.HIGHEST)]
    reshape x3 -> x0, local copies, waits for them, and re-layouts: 14.3 us -> none  [the longest x2 11.2 us: on_device(): intra_out = jnp.einsum('bhts,bshp->bthp', intra_weights, value_blocks.res...]
  transfers between devices with their start and end apart: 10 -> 0, of which waited for: 10 -> 0; matrix products, arithmetic and copies ran while one was open for 5% -> 0% of each run, Pallas kernels for 0% -> 0%
where the time goes in v2:
time: 133 us; the launch traced here: 132 us
  Pallas kernels  129 us (97%)
  local copies, waits for them, and re-layouts  3.1 us (2%)
    pallas_call x1, Pallas kernels, on_device(): pl.pallas_call(kernel, out_shape=jax.ShapeDtypeStruct((tokens, full), jnp...  129 us
    unnamed x12, local copies, waits for them, and re-layouts  3.1 us

profile of v2, /device:TPU:1, one launch (start us, length us, event | category | flops | bytes accessed | tf_op | source)
XLA Modules:
  0.0 132.1 jit_solution(2268950392336453800)
XLA Ops:
  0.0 0.0 copy-start.1
  0.0 0.0 copy-start.2
  0.0 0.0 copy-start.3
  0.0 0.0 copy-start.4
  0.0 0.9 copy.7.dt_ref
  0.9 0.0 copy-done.1
  0.9 0.0 copy-done.2
  0.9 0.0 copy-done.3
  0.9 0.0 copy-done.4
  1.0 0.0 copy-start
  1.0 1.2 copy-done
  2.2 128.9 %shard_map.64 = bf16[128,4096]{1,0:T(8,128)(2,1)S(1)} custom-call(bf16[128,4096]{1,0:T(8,128)(2,1)S(1)} %copy-done, bf16[128,128]{1,0:T(8,128)(2,1)S(1)} %copy-done.1, bf16[128,128]{1,0:T(8,128)(2,1)S(1)} %copy-done.2, f32[128,64]{1,0:T(8,128)S(1)} %copy.7.dt_ref, f32[20,64]{1,0:T(8,128)S(1)} %copy-done.3, f32[1,64]{1,0:T(1,128)S(1)} %bitcast.1), custom_call_target="tpu_custom_call" | custom-call | flops 671088640 | bytes 2097152 | tf_op jit(solution)/shard_map/pallas_call | solution.py:435
  131.1 1.0 copy.9
Async XLA Ops:
  0.0 0.9 copy-start.1
  0.0 0.9 copy-start.2
  0.0 0.9 copy-start.3
  0.0 0.9 copy-start.4
  1.0 1.2 copy-start

commit v3 on v2

--- a/solution.py
+++ b/solution.py
@@ -275,7 +275,6 @@
         plane_start(0)
         for p in sums[6:]:
             sum_step(p)
-        later(0)
         plane_own(0)
         spread(0, owner)
         plane_start(1)
@@ -284,7 +283,6 @@
         plane_own(1)
         for p in backs[2:4]:
             back_step(p)
-        later(1)
         spread(1, owner)
         for p in backs[4:]:
             back_step(p)
@@ -300,6 +298,8 @@
     @pl.when(spot == 0)
     def _():
         for p in SUM_UP:
+            send_up(p, state.at[at(p)])
+        for p in BACK_UP:
             send_up(p, state.at[at(p)])
         local_part()
 

time: 133 us -> 125 us (0.940)
  the two profiles are of different devices: /device:TPU:1 before, /device:TPU:4 now
where the time goes in v3:
time: 125 us
  Pallas kernels  121 us (97%)
  local copies, waits for them, and re-layouts  3.1 us (2%)
    pallas_call x1, Pallas kernels, on_device(): pl.pallas_call(kernel, out_shape=jax.ShapeDtypeStruct((tokens, full), jnp...  121 us
    unnamed x12, local copies, waits for them, and re-layouts  3.1 us

profile of v3, /device:TPU:4, one launch (start us, length us, event | category | flops | bytes accessed | tf_op | source)
XLA Modules:
  0.0 124.7 jit_solution(16357142793353020962)
XLA Ops:
  0.0 0.0 copy-start.1
  0.0 0.0 copy-start.2
  0.0 0.0 copy-start.3
  0.0 0.0 copy-start.4
  0.0 0.9 copy.7.dt_ref
  0.9 0.0 copy-done.1
  0.9 0.0 copy-done.2
  0.9 0.0 copy-done.3
  0.9 0.0 copy-done.4
  1.0 0.0 copy-start
  1.0 1.2 copy-done
  2.2 121.5 %shard_map.64 = bf16[128,4096]{1,0:T(8,128)(2,1)S(1)} custom-call(bf16[128,4096]{1,0:T(8,128)(2,1)S(1)} %copy-done, bf16[128,128]{1,0:T(8,128)(2,1)S(1)} %copy-done.1, bf16[128,128]{1,0:T(8,128)(2,1)S(1)} %copy-done.2, f32[128,64]{1,0:T(8,128)S(1)} %copy.7.dt_ref, f32[20,64]{1,0:T(8,128)S(1)} %copy-done.3, f32[1,64]{1,0:T(1,128)S(1)} %bitcast.1), custom_call_target="tpu_custom_call" | custom-call | flops 671088640 | bytes 2097152 | tf_op jit(solution)/shard_map/pallas_call | solution.py:435
  123.7 1.0 copy.9
Async XLA Ops:
  0.0 0.9 copy-start.1
  0.0 0.9 copy-start.2
  0.0 0.9 copy-start.3
  0.0 0.9 copy-start.4
  1.0 1.2 copy-start

commit v4 on v3

--- a/solution.py
+++ b/solution.py
@@ -11,7 +11,7 @@
 GROUP = 4
 PIECES = 16
 HALF = 8
-LEAD = 2
+LEAD = 1
 TILE = 512
 SUM_UP = (14, 12, 10, 8, 15, 13, 11, 9)
 SUM_DOWN = (0, 2, 4, 6, 1, 3, 5, 7)
@@ -269,7 +269,7 @@
     def put(p, value):
         level[at(p), :] = value
 
-    def end_chip(owner, sums, sum_step, later, backs, back_step):
+    def end_chip(owner, sums, sum_step, backs, back_step):
         for p in sums[:6]:
             sum_step(p)
         plane_start(0)
@@ -278,10 +278,8 @@
         plane_own(0)
         spread(0, owner)
         plane_start(1)
-        for p in backs[:2]:
-            back_step(p)
         plane_own(1)
-        for p in backs[2:4]:
+        for p in backs[:4]:
             back_step(p)
         spread(1, owner)
         for p in backs[4:]:
@@ -297,25 +295,19 @@
 
     @pl.when(spot == 0)
     def _():
-        for p in SUM_UP:
-            send_up(p, state.at[at(p)])
-        for p in BACK_UP:
+        for p in SUM_UP + BACK_UP:
             send_up(p, state.at[at(p)])
         local_part()
 
         def sum_step(p):
             group_sum(p, state[at(p), :] + get_down(p))
-
-        def later(half):
-            for p in BACK_UP[4 * half : 4 * half + 4]:
-                send_up(p, state.at[at(p)])
 
         def back_step(p):
             value = get_base(p)
             send_up(PIECES + p % HALF, base.at[p % HALF])
             put(p, value)
 
-        end_chip(0, SUM_DOWN, sum_step, later, BACK_UP, back_step)
+        end_chip(0, SUM_DOWN, sum_step, BACK_UP, back_step)
         for r in BACK_DOWN:
             put(r, get_down(r))
 
@@ -329,12 +321,12 @@
             group_sum(p, state[at(p), :] + get_up(p))
 
         def back_step(r):
-            value = get_base(r)
+            get_base(r)
             send_down(r, base.at[r % HALF])
-            put(r, value + get_up(PIECES + r % HALF))
-
-        end_chip(3, SUM_UP, sum_step, lambda half: None, BACK_DOWN, back_step)
-        for p in BACK_UP:
+
+        end_chip(3, SUM_UP, sum_step, BACK_DOWN, back_step)
+        for p, r in zip(BACK_UP, BACK_DOWN):
+            put(r, base[r % HALF] + get_up(PIECES + r % HALF))
             put(p, get_up(p))
 
     w0, w1 = weight(1), weight(2)

time: 125 us -> 119 us (0.952)
  the two profiles are of different devices: /device:TPU:4 before, /device:TPU:1 now
where the time goes in v4:
time: 119 us; the launch traced here: 118 us
  Pallas kernels  115 us (97%)
  local copies, waits for them, and re-layouts  3.1 us (3%)
    pallas_call x1, Pallas kernels, on_device(): pl.pallas_call(kernel, out_shape=jax.ShapeDtypeStruct((tokens, full), jnp...  115 us
    unnamed x12, local copies, waits for them, and re-layouts  3.1 us

profile of v4, /device:TPU:1, one launch (start us, length us, event | category | flops | bytes accessed | tf_op | source)
XLA Modules:
  0.0 118.0 jit_solution(14766387512392310084)
XLA Ops:
  0.0 0.0 copy-start.1
  0.0 0.0 copy-start.2
  0.0 0.0 copy-start.3
  0.0 0.0 copy-start.4
  0.0 0.9 copy.7.dt_ref
  0.9 0.0 copy-done.1
  0.9 0.0 copy-done.2
  0.9 0.0 copy-done.3
  0.9 0.0 copy-done.4
  1.0 0.0 copy-start
  1.0 1.2 %copy-done = bf16[128,4096]{1,0:T(8,128)(2,1)S(1)} copy-done((bf16[128,4096]{1,0:T(8,128)(2,1)S(1)}, bf16[128,4096]{1,0:T(8,128)(2,1)}, u32[]{:S(2)}) %copy-start) | copy-done | bytes 1048600
  2.2 114.8 %shard_map.64 = bf16[128,4096]{1,0:T(8,128)(2,1)S(1)} custom-call(bf16[128,4096]{1,0:T(8,128)(2,1)S(1)} %copy-done, bf16[128,128]{1,0:T(8,128)(2,1)S(1)} %copy-done.1, bf16[128,128]{1,0:T(8,128)(2,1)S(1)} %copy-done.2, f32[128,64]{1,0:T(8,128)S(1)} %copy.7.dt_ref, f32[20,64]{1,0:T(8,128)S(1)} %copy-done.3, f32[1,64]{1,0:T(1,128)S(1)} %bitcast.1), custom_call_target="tpu_custom_call" | custom-call | flops 671088640 | bytes 2097152 | tf_op jit(solution)/shard_map/pallas_call | solution.py:427
  117.0 1.0 copy.9
Async XLA Ops:
  0.0 0.9 copy-start.1
  0.0 0.9 copy-start.2
  0.0 0.9 copy-start.3
  0.0 0.9 copy-start.4
  1.0 1.2 %copy-start = (bf16[128,4096]{1,0:T(8,128)(2,1)S(1)}, bf16[128,4096]{1,0:T(8,128)(2,1)}, u32[]{:S(2)}) copy-start(bf16[128,4096]{1,0:T(8,128)(2,1)} %x_ref.1) | copy-start | bytes 3145732

commit v5 on v4

--- a/solution.py
+++ b/solution.py
@@ -270,10 +270,10 @@
         level[at(p), :] = value
 
     def end_chip(owner, sums, sum_step, backs, back_step):
-        for p in sums[:6]:
+        for p in sums[:5]:
             sum_step(p)
         plane_start(0)
-        for p in sums[6:]:
+        for p in sums[5:]:
             sum_step(p)
         plane_own(0)
         spread(0, owner)
@@ -380,7 +380,7 @@
             send_up(p, out_up.at[p])
             put(p, value)
 
-        in_turn(each(back_down, BACK_DOWN), each(back_up, BACK_UP), LEAD)
+        in_turn(each(back_down, BACK_DOWN), each(back_up, BACK_UP), LEAD + 1)
 
     q_turned = product(q_ref[...], turn).astype(jnp.bfloat16)
 

time: 119 us -> 119 us (level)
  no operation moved by 1% of the time
where the time goes in v5:
time: 119 us
  Pallas kernels  115 us (97%)
  local copies, waits for them, and re-layouts  3.1 us (3%)
    pallas_call x1, Pallas kernels, on_device(): pl.pallas_call(kernel, out_shape=jax.ShapeDtypeStruct((tokens, full), jnp...  115 us
    unnamed x12, local copies, waits for them, and re-layouts  3.1 us

profile of v5, /device:TPU:1, one launch (start us, length us, event | category | flops | bytes accessed | tf_op | source)
XLA Modules:
  0.0 118.6 jit_solution(7319877280893733035)
XLA Ops:
  0.0 0.0 copy-start.1
  0.0 0.0 copy-start.2
  0.0 0.0 copy-start.3
  0.0 0.0 copy-start.4
  0.0 0.9 copy.7.dt_ref
  0.9 0.0 copy-done.1
  0.9 0.0 copy-done.2
  0.9 0.0 copy-done.3
  0.9 0.0 copy-done.4
  1.0 0.0 copy-start
  1.0 1.2 %copy-done = bf16[128,4096]{1,0:T(8,128)(2,1)S(1)} copy-done((bf16[128,4096]{1,0:T(8,128)(2,1)S(1)}, bf16[128,4096]{1,0:T(8,128)(2,1)}, u32[]{:S(2)}) %copy-start) | copy-done | bytes 1048600
  2.2 115.4 %shard_map.64 = bf16[128,4096]{1,0:T(8,128)(2,1)S(1)} custom-call(bf16[128,4096]{1,0:T(8,128)(2,1)S(1)} %copy-done, bf16[128,128]{1,0:T(8,128)(2,1)S(1)} %copy-done.1, bf16[128,128]{1,0:T(8,128)(2,1)S(1)} %copy-done.2, f32[128,64]{1,0:T(8,128)S(1)} %copy.7.dt_ref, f32[20,64]{1,0:T(8,128)S(1)} %copy-done.3, f32[1,64]{1,0:T(1,128)S(1)} %bitcast.1), custom_call_target="tpu_custom_call" | custom-call | flops 671088640 | bytes 2097152 | tf_op jit(solution)/shard_map/pallas_call | solution.py:427
  117.6 1.0 copy.9
Async XLA Ops:
  0.0 0.9 copy-start.1
  0.0 0.9 copy-start.2
  0.0 0.9 copy-start.3
  0.0 0.9 copy-start.4
  1.0 1.2 %copy-start = (bf16[128,4096]{1,0:T(8,128)(2,1)S(1)}, bf16[128,4096]{1,0:T(8,128)(2,1)}, u32[]{:S(2)}) copy-start(bf16[128,4096]{1,0:T(8,128)(2,1)} %x_ref.1) | copy-start | bytes 3145732

commit v6 on v5

--- a/solution.py
+++ b/solution.py
@@ -383,6 +383,7 @@
         in_turn(each(back_down, BACK_DOWN), each(back_up, BACK_UP), LEAD + 1)
 
     q_turned = product(q_ref[...], turn).astype(jnp.bfloat16)
+    q_twice = jnp.concatenate([q_turned, q_turned], axis=1)
 
     def finish(t, carry):
         cols = columns(t)
@@ -390,7 +391,7 @@
         high_part = found.astype(jnp.bfloat16)
         low_part = (found - high_part.astype(jnp.float32)).astype(jnp.bfloat16)
         o_ref[:, cols] = (
-            acc[:, cols] + product(q_turned, high_part) + product(q_turned, low_part)
+            acc[:, cols] + product(q_twice, jnp.concatenate([high_part, low_part], axis=0))
         ).astype(o_ref.dtype)
         return carry
 

time: 119 us -> 119 us (level)
  no operation moved by 1% of the time
where the time goes in v6:
time: 119 us; the launch traced here: 118 us
  Pallas kernels  115 us (97%)
  local copies, waits for them, and re-layouts  3.1 us (3%)
    pallas_call x1, Pallas kernels, on_device(): pl.pallas_call(kernel, out_shape=jax.ShapeDtypeStruct((tokens, full), jnp...  115 us
    unnamed x12, local copies, waits for them, and re-layouts  3.1 us

profile of v6, /device:TPU:1, one launch (start us, length us, event | category | flops | bytes accessed | tf_op | source)
XLA Modules:
  0.0 118.4 jit_solution(1419428224212990687)
XLA Ops:
  0.0 0.0 copy-start.1
  0.0 0.0 copy-start.2
  0.0 0.0 copy-start.3
  0.0 0.0 copy-start.4
  0.0 0.9 copy.7.dt_ref
  0.9 0.0 copy-done.1
  0.9 0.0 copy-done.2
  0.9 0.0 copy-done.3
  0.9 0.0 copy-done.4
  1.0 0.0 copy-start
  1.0 1.2 %copy-done = bf16[128,4096]{1,0:T(8,128)(2,1)S(1)} copy-done((bf16[128,4096]{1,0:T(8,128)(2,1)S(1)}, bf16[128,4096]{1,0:T(8,128)(2,1)}, u32[]{:S(2)}) %copy-start) | copy-done | bytes 1048600
  2.2 115.2 %shard_map.64 = bf16[128,4096]{1,0:T(8,128)(2,1)S(1)} custom-call(bf16[128,4096]{1,0:T(8,128)(2,1)S(1)} %copy-done, bf16[128,128]{1,0:T(8,128)(2,1)S(1)} %copy-done.1, bf16[128,128]{1,0:T(8,128)(2,1)S(1)} %copy-done.2, f32[128,64]{1,0:T(8,128)S(1)} %copy.7.dt_ref, f32[20,64]{1,0:T(8,128)S(1)} %copy-done.3, f32[1,64]{1,0:T(1,128)S(1)} %bitcast.1), custom_call_target="tpu_custom_call" | custom-call | flops 671088640 | bytes 2097152 | tf_op jit(solution)/shard_map/pallas_call | solution.py:428
  117.4 1.0 copy.9
Async XLA Ops:
  0.0 0.9 copy-start.1
  0.0 0.9 copy-start.2
  0.0 0.9 copy-start.3
  0.0 0.9 copy-start.4
  1.0 1.2 %copy-start = (bf16[128,4096]{1,0:T(8,128)(2,1)S(1)}, bf16[128,4096]{1,0:T(8,128)(2,1)}, u32[]{:S(2)}) copy-start(bf16[128,4096]{1,0:T(8,128)(2,1)} %x_ref.1) | copy-start | bytes 3145732
